TPU v7x, 768 devices: a whole 4x8x12 slice. The times are simulated.
768 devices in a mesh: grp: 16 (over x, y_lo), shard: 48 (over z, y_hi, core).
Axes of the slice: x: 4, y: 8 (y_hi: 2, y_lo: 4; y = y_hi * 4 + y_lo), z: 12, core: 2. Of those that a mesh axis runs over, the one named last changes fastest.
Arguments:
- hidden: bfloat16 [6144, 4096], P(('grp', 'shard')), may hold values from -160 to 160
- norm_gain: float32 [4096], replicated, may hold values from 0.5 to 1.5
- gate_codes: bfloat16 [4096, 7296], P('grp', 'shard'), may hold values from -6 to 6
- gate_scales: float32 [32, 7296], P('grp', 'shard'), may hold values from 0.005 to 0.05
- up_codes: bfloat16 [4096, 7296], P('grp', 'shard'), may hold values from -6 to 6
- up_scales: float32 [32, 7296], P('grp', 'shard'), may hold values from 0.005 to 0.05
- down_codes: bfloat16 [4096, 7296], P('grp', 'shard'), may hold values from -6 to 6
- down_scales: float32 [32, 7296], P('grp', 'shard'), may hold values from 0.0058536613 to 0.05853661
- head: bfloat16 [4096, 100], replicated, may hold values from -1 to 1
- teacher: float32 [6144, 100], P('grp'), may hold values from -400 to 400
- targets: int32 [6144], P('grp'), may hold values from 0 to 99
Outputs:
- loss: float32 [6144], P(('grp', 'shard'))
- grad_gate: float32 [4096, 7296], P('grp', 'shard')
- grad_up: float32 [4096, 7296], P('grp', 'shard')
- grad_down: float32 [4096, 7296], P('grp', 'shard')
All inputs are finite; a program needn't handle non-finite values.
Results may differ from a plain program's by a relative error of at most 0.023.
Values may be sent and summed in bfloat16 or wider, within the bound.
A program may use at most 32 MiB of HBM per device.

v0:
```python
import jax
import jax.numpy as jnp
from jax import lax
from jax.sharding import PartitionSpec as P

eps = 1e-05
loss_scale = 64.0


def dequantize(codes, scales):
    rows, cols = codes.shape
    blocks = scales.shape[0]
    scaled = codes.astype(jnp.float32).reshape(blocks, rows // blocks, cols) * scales[:, None, :]
    return scaled.reshape(rows, cols).astype(jnp.bfloat16)


def log_softmax_rows(values):
    top = jnp.max(values, axis=1, keepdims=True)
    shifted = values - top
    return shifted - jnp.log(jnp.sum(jnp.exp(shifted), axis=1, keepdims=True))


def weight_term(left, right):
    return jnp.einsum("rd,rf->df", left, right, preferred_element_type=jnp.float32)


def local(
    hidden,
    norm_gain,
    gate_codes,
    gate_scales,
    up_codes,
    up_scales,
    down_codes,
    down_scales,
    head,
    teacher,
    targets,
):
    own_rows = hidden.shape[0]
    offset = lax.axis_index("shard") * own_rows
    x_float = hidden.astype(jnp.float32)
    normed = (
        x_float * lax.rsqrt(jnp.mean(x_float * x_float, axis=1, keepdims=True) + eps) * norm_gain
    ).astype(jnp.bfloat16)
    gathered = lax.all_gather(normed, "shard", axis=0, tiled=True)
    w_gate = dequantize(gate_codes, gate_scales)
    w_up = dequantize(up_codes, up_scales)
    w_down = dequantize(down_codes, down_scales)
    width = w_gate.shape[1]
    head_float = head.astype(jnp.float32)
    sliced = gathered
    gate = jnp.dot(
        sliced,
        lax.all_gather(w_gate, "grp", axis=0, tiled=True),
        preferred_element_type=jnp.float32,
    )
    up = jnp.dot(
        sliced, lax.all_gather(w_up, "grp", axis=0, tiled=True), preferred_element_type=jnp.float32
    )
    sig = jax.nn.sigmoid(gate)
    act = gate * sig
    units = (act * up).astype(jnp.bfloat16)
    branch_part = jnp.einsum(
        "rf,df->rd",
        units,
        lax.all_gather(w_down, "grp", axis=0, tiled=True),
        preferred_element_type=jnp.float32,
    )
    partial_value = jnp.dot(branch_part, head_float, precision=lax.Precision.HIGHEST)
    own_logits = jnp.dot(hidden, head, preferred_element_type=jnp.float32)
    placed = lax.dynamic_slice_in_dim(partial_value, offset, own_rows, 0) + own_logits
    partial_value = lax.dynamic_update_slice_in_dim(partial_value, placed, offset, 0)
    logits = lax.psum(partial_value, "shard")
    log_student = log_softmax_rows(logits)
    log_teacher = log_softmax_rows(teacher)
    p_student = jnp.exp(log_student)
    p_teacher = jnp.exp(log_teacher)
    onehot = (jnp.arange(head.shape[1], dtype=jnp.int32)[None, :] == targets[:, None]).astype(
        jnp.float32
    )
    loss = -jnp.sum(onehot * log_student, axis=1) + jnp.sum(
        p_teacher * (log_teacher - log_student), axis=1
    )
    d_logits = loss_scale * (2.0 * p_student - onehot - p_teacher)
    d_branch = jnp.dot(d_logits, head_float.T, precision=lax.Precision.HIGHEST).astype(jnp.bfloat16)
    sliced = d_branch
    d_units = jnp.dot(
        sliced,
        lax.all_gather(w_down, "grp", axis=0, tiled=True),
        preferred_element_type=jnp.float32,
    )
    d_gate = (d_units * up * sig * (1.0 + gate * (1.0 - sig))).astype(jnp.bfloat16)
    d_up = (d_units * act).astype(jnp.bfloat16)
    summed = lax.psum_scatter(
        jnp.concatenate(
            [
                weight_term(gathered, d_gate),
                weight_term(gathered, d_up),
                weight_term(d_branch, units),
            ],
            axis=1,
        ).astype(jnp.bfloat16),
        "grp",
        scatter_dimension=0,
        tiled=True,
    ).astype(jnp.float32)
    grad_gate = summed[:, :width]
    grad_up = summed[:, width : 2 * width]
    grad_down = summed[:, 2 * width :]
    loss_own = lax.dynamic_slice_in_dim(loss, offset, own_rows, 0)
    return (loss_own, grad_gate, grad_up, grad_down)


def solution(mesh):
    in_specs = (
        P(("grp", "shard"), None),
        P(),
        P("grp", "shard"),
        P("grp", "shard"),
        P("grp", "shard"),
        P("grp", "shard"),
        P("grp", "shard"),
        P("grp", "shard"),
        P(),
        P("grp", None),
        P("grp"),
    )
    out_specs = (P(("grp", "shard")), P("grp", "shard"), P("grp", "shard"), P("grp", "shard"))
    return jax.shard_map(local, mesh=mesh, in_specs=in_specs, out_specs=out_specs, check_vma=False)
```

profile of v0, /device:TPU:1, one launch (start us, length us, event | category | flops | bytes accessed | tf_op | source)
XLA Modules:
  0.0 979.7 jit_solution(4772147302221044675)
XLA Ops:
  7.2 0.0 all-gather.7.cloned.1.call-start
  7.2 0.8 copy.15
  8.1 0.2 mul.99
  8.3 1.5 fusion.9
  9.9 0.0 all-gather.7.cloned.1.call-update
  9.9 0.0 all-gather.5.cloned.1.call-start
  9.9 1.0 fusion.13
  10.9 1.6 fusion.15
  12.5 0.0 all-gather.5.cloned.1.call-update
  12.5 0.0 all-gather.9.cloned.1.call-start
  12.6 0.8 copy.16
  13.3 0.2 mul.103
  13.6 1.5 fusion.8
  15.1 0.0 all-gather.9.cloned.1.call-update
  15.1 0.0 all-gather.11.cloned.1.call-start
  15.2 0.8 copy.17
  16.0 0.2 mul.107
  16.2 1.5 fusion.7
  17.8 0.0 all-reduce.2.cloned.1.call-start
  17.8 71.1 %all-gather.7.cloned.1.call-done = bf16[4096,152]{0,1:T(8,128)(2,1)} async-done(((bf16[256,152]{0,1:T(8,128)(2,1)}), bf16[4096,152]{0,1:T(8,128)(2,1)}) %all-gather.7.cloned.1.call-update) | async-done | bytes 1245200 | tf_op jit(solution)/shard_map/all_gather | solution.py:55
  88.9 143.3 %all-gather.5.cloned.1.call-done = bf16[384,4096]{1,0:T(8,128)(2,1)} async-done(((bf16[8,4096]{1,0:T(8,128)(2,1)}), bf16[384,4096]{1,0:T(8,128)(2,1)}) %all-gather.5.cloned.1.call-update) | async-done | bytes 3145744 | tf_op jit(solution)/shard_map/all_gather | solution.py:46
  232.2 3.3 fusion.30
  235.6 64.7 %all-gather.9.cloned.1.call-done = bf16[4096,152]{0,1:T(8,128)(2,1)} async-done(((bf16[256,152]{0,1:T(8,128)(2,1)}), bf16[4096,152]{0,1:T(8,128)(2,1)}) %all-gather.9.cloned.1.call-update) | async-done | bytes 1245200 | tf_op jit(solution)/shard_map/all_gather | solution.py:59
  300.3 3.3 multiply_convert_fusion.2
  303.6 77.3 %all-gather.11.cloned.1.call-done = bf16[4096,152]{0,1:T(8,128)(2,1)} async-done(((bf16[256,152]{0,1:T(8,128)(2,1)}), bf16[4096,152]{0,1:T(8,128)(2,1)}) %all-gather.11.cloned.1.call-update) | async-done | bytes 1245200 | tf_op jit(solution)/shard_map/all_gather | solution.py:67
  380.9 2.3 fusion.31
  383.2 3.3 fusion.32
  386.6 0.4 convolution_add_fusion
  386.9 0.8 dynamic_update_slice.3
  387.7 0.7 copy-done.5
  388.4 0.2 reduce-scatter.2.cloned.1.call-start
  388.7 0.1 exponential_reduce_fusion
  388.7 476.6 %all-reduce.2.cloned.1.call-done = f32[384,100]{0,1:T(8,128)} async-done(((f32[384,100]{0,1:T(8,128)}), f32[384,100]{0,1:T(8,128)}) %all-reduce.2.cloned.1.call-update) | async-done | bytes 153616 | tf_op jit(solution)/shard_map/psum | solution.py:74
  865.3 0.9 reduce_max.18
  866.3 1.0 exponential_reduce_fusion.1
  867.2 3.9 convolution_convert_fusion
  871.1 0.8 convolution_convert_fusion.1
  871.9 0.5 copy-done.2
  872.4 1.1 fusion.33
  873.6 0.7 copy-done.1
  874.3 0.8 convolution_convert_fusion.2
  875.1 0.8 convolution_convert_fusion.3
  876.0 2.1 pad_maximum_fusion
  878.1 0.9 copy-done.4
  879.0 0.1 select_reduce_fusion
  879.1 0.6 dynamic_slice.7
  879.7 91.5 %reduce-scatter.2.cloned.1.call-done = bf16[256,456]{0,1:T(8,128)(2,1)} async-done(((bf16[4096,456]{0,1:T(8,128)(2,1)}), bf16[256,456]{0,1:T(8,128)(2,1)}) %reduce-scatter.2.cloned.1.call-update) | async-done | bytes 233488 | tf_op jit(solution)/shard_map/reduce_scatter | solution.py:95
  971.2 1.7 fusion.29
  (20 shorter events, 0.1 us)
Async XLA Ops:
  7.2 376.0 %copy-start = (bf16[4096,100]{0,1:T(8,128)(2,1)S(1)}, bf16[4096,100]{0,1:T(8,128)(2,1)}, u32[]{:S(2)}) copy-start(bf16[4096,100]{0,1:T(8,128)(2,1)} %param.19) | copy-start | bytes 2457604
  7.2 81.7 %all-gather.7.cloned.1.call-start = ((), (), s32[]{:S(2)}) async-start(), calls=%async_computation.2 | async-start | bytes 1323008 | tf_op jit(solution)/shard_map/all_gather | solution.py:55
  9.9 222.4 %all-gather.5.cloned.1.call-start = ((), (), s32[]{:S(2)}) async-start(), calls=%async_computation.1 | async-start | bytes 3211264 | tf_op jit(solution)/shard_map/all_gather | solution.py:46
  12.5 287.8 %all-gather.9.cloned.1.call-start = ((), (), s32[]{:S(2)}) async-start(), calls=%async_computation.3 | async-start | bytes 1323008 | tf_op jit(solution)/shard_map/all_gather | solution.py:59
  15.1 365.7 %all-gather.11.cloned.1.call-start = ((), (), s32[]{:S(2)}) async-start(), calls=%async_computation.4 | async-start | bytes 1323008 | tf_op jit(solution)/shard_map/all_gather | solution.py:67
  17.8 847.5 %all-reduce.2.cloned.1.call-start = ((), (), s32[]{:S(2)}) async-start(), calls=%async_computation.5 | async-start | bytes 319488 | tf_op jit(solution)/shard_map/psum | solution.py:74
  383.2 3.3 copy-start.6
  383.2 5.4 copy-start.3
  383.2 484.0 %copy-start.7 = (s32[384]{0:T(512)S(1)}, s32[384]{0:T(512)}, u32[]{:S(2)}) copy-start(s32[384]{0:T(512)} %param.21) | copy-start | bytes 4612
  387.7 0.7 copy-start.5
  388.4 582.8 %reduce-scatter.2.cloned.1.call-start = ((), (), s32[]{:S(2)}) async-start(), calls=%async_computation.6 | async-start | bytes 3969024 | tf_op jit(solution)/shard_map/reduce_scatter | solution.py:95
  871.1 1.3 copy-start.2
  872.4 1.9 copy-start.1
  878.1 0.9 copy-start.4
Sparse Core Ops, SparseCore 0:
  10.9 77.9 all-gather.6
  92.6 139.6 all-gather.4
  235.1 65.1 all-gather.8
  303.0 77.8 all-gather.10
  388.5 476.7 all-reduce.1
  878.2 92.8 reduce-scatter.1
where the time goes:
time: 989 us; the launch traced here: 980 us
  waiting for transfers between devices  925 us (94%)
  matrix products  20.1 us (2%)
  between operations  14.3 us (1%)
  other arithmetic  11.4 us (1%)
    psum x1, waiting for transfers between devices, local(): logits = lax.psum(partial_value, 'shard')  477 us
    all_gather x1, waiting for transfers between devices, local(): gathered = lax.all_gather(normed, 'shard', axis=0, tiled=True)  143 us
    reduce_scatter x1, waiting for transfers between devices, local(): lax.psum_scatter(jnp.concatenate([weight_term(gathered, d_gate), weight_t...  91.5 us
    all_gather x1, waiting for transfers between devices, local(): lax.all_gather(w_down, 'grp', axis=0, tiled=True)  77.3 us
    all_gather x1, waiting for transfers between devices, local(): lax.all_gather(w_gate, 'grp', axis=0, tiled=True)  71.1 us
    all_gather x1, waiting for transfers between devices, local(): lax.all_gather(w_up, 'grp', axis=0, tiled=True)  64.7 us
  transfers between devices with their start and end apart: 6, of which 6 were waited for; matrix products, arithmetic and copies ran while one was open for 2% of the time, Pallas kernels for 0%

commit v1 on v0

v1 whole, which is shorter than its diff:
```python
import functools

import jax
import jax.numpy as jnp
from jax import lax
from jax.experimental import pallas as pl
from jax.experimental.pallas import tpu as pltpu
from jax.sharding import PartitionSpec as P

eps = 1e-05
loss_scale = 64.0
MESH = pl.DeviceIdType.MESH
f32, bf16 = jnp.float32, jnp.bfloat16

X, Y = 4, 4
H, C = 2, 2
CUT = 160
LANES = 128


def nt(left, right):
    return lax.dot_general(left, right, (((1,), (1,)), ((), ())), preferred_element_type=f32)


def nn(left, right):
    return jnp.dot(left, right, preferred_element_type=f32)


def tn(left, right):
    return lax.dot_general(left, right, (((0,), (0,)), ((), ())), preferred_element_type=f32)


def split(value):
    high = value.astype(bf16)
    return high, (value - high.astype(f32)).astype(bf16)


class Wires:
    def __init__(self, send_sems, recv_sems, names):
        self.send_sems, self.recv_sems, self.names, self.started = send_sems, recv_sems, names, []

    def slot(self, name):
        return self.names[name]

    def describe(self, name, src, dst, device):
        at = self.slot(name)
        return pltpu.make_async_remote_copy(
            src_ref=src,
            dst_ref=dst,
            send_sem=self.send_sems.at[at],
            recv_sem=self.recv_sems.at[at],
            device_id=device,
            device_id_type=MESH,
        )

    def send(self, name, src, dst, device):
        copy = self.describe(name, src, dst, device)
        copy.start()
        self.started.append(copy)

    def recv(self, name, dst, device):
        self.describe(name, dst, dst, device).wait_recv()

    def finish(self):
        for copy in self.started:
            copy.wait_send()


def wire_names(Z):
    half = Z // 2
    names = ["e", "hx", "l1", "l3", "l5"]
    for j in range(Y):
        names += [f"{kind}{j}" for kind in ("y", "xp", "xm", "fp", "fm", "ra", "rb", "sp", "sm", "ry")]
    for s in range(2):
        for n in range(1, half + 1):
            names += [f"zp{s}_{n}", f"zm{s}_{n}"]
        for k in range(-half, half + 1):
            names.append(f"c{s}_{k}")
    for k in range(1, Z):
        names += [f"l2_{k}", f"l4_{k}"]
    for kind in ("m", "n"):
        for k in range(1, X):
            names += [f"{kind}r{k}", f"{kind}a{k}"]
        for j in range(1, Y):
            names.append(f"{kind}y{j}")
    return {name: at for at, name in enumerate(names)}


def kernel(
    names, Z, D, F, B,
    hid, gain, gc, gs, uc, us, dc, ds, head, teach, targ,
    loss_o, gg_o, gu_o, gd_o,
    halves, pair, nb, wt, scale_pad, head_own, own_logit, teach_pad, teach_rows,
    acc, units_s, whole, mred, mrx, mry, nred, nrx, nry,
    part, l1_in, summed, l2_in, l3_out, l3_in, dl, loss_s,
    grads, ra, rb, sp, sm, ry,
    send_sems, recv_sems,
):
    grp, sh = lax.axis_index("grp"), lax.axis_index("shard")
    x, y = lax.div(grp, Y), lax.rem(grp, Y)
    z, h, c = lax.div(sh, H * C), lax.rem(lax.div(sh, C), H), lax.rem(sh, C)
    half = Z // 2
    RB = D // (X * Y)
    T8 = hid.shape[0]
    KH = D // 2

    def xat(dx):
        return lax.rem(x + dx % X, X) if dx % X else x

    def yat(j):
        return (y, y + 1 - 2 * lax.rem(y, 2), y + 2 - 4 * lax.div(y, 2), 3 - y)[j]

    def zat(dz):
        return lax.rem(z + dz % Z, Z) if dz % Z else z

    def to_x(dx):
        return {"grp": xat(dx) * Y + y}

    def to_y(j):
        return {"grp": x * Y + yat(j)}

    def to_z(dz):
        return {"shard": (zat(dz) * H + h) * C + c}

    to_h = {"shard": (z * H + (1 - h)) * C + c}
    to_c = {"shard": (z * H + h) * C + (1 - c)}

    wires = Wires(send_sems, recv_sems, names)
    send, recv = wires.send, wires.recv

    barrier = pltpu.get_barrier_semaphore()
    peers = [to_c, to_h] + [to_x(k) for k in range(1, X)] + [to_y(j) for j in range(1, Y)]
    peers += [to_z(k) for k in range(1, Z)]
    for peer in peers:
        pl.semaphore_signal(barrier, inc=1, device_id=peer, device_id_type=MESH)

    xf = hid[...].astype(f32)
    mean = jnp.mean(xf * xf, axis=1, keepdims=True)
    normed = (xf * lax.rsqrt(mean + eps) * gain[...]).astype(bf16).astype(f32)
    halves[0] = normed[:, :KH]
    halves[1] = normed[:, KH:]
    pair[c] = halves[c]

    scale_pad[...] = jnp.zeros_like(scale_pad)
    scale_pad[0:2, 0:F] = gs[...]
    scale_pad[8:10, 0:F] = us[...]
    scale_pad[16:18, 0:F] = ds[...]
    columns = scale_pad[...].T

    def dequantize(codes, at):
        value = codes[...].astype(f32)
        mid = RB // 2
        left = value[:, :mid] * columns[:F, at : at + 1]
        right = value[:, mid:] * columns[:F, at + 1 : at + 2]
        return jnp.concatenate([left, right], axis=1)

    wt[grp] = jnp.concatenate([dequantize(gc, 0), dequantize(uc, 8)], axis=0).astype(bf16)

    pl.semaphore_wait(barrier, len(peers))

    send("e", halves.at[1 - c], pair.at[c], to_c)
    send("xp0", wt.at[grp], wt.at[grp], to_x(1))
    send("xm0", wt.at[grp], wt.at[grp], to_x(-1))
    for j in range(1, Y):
        send(f"y{j}", wt.at[grp], wt.at[grp], to_y(j))

    def gat(dx, j):
        return xat(dx) * Y + yat(j)

    def spread_y(j):
        block = wt.at[gat(0, j)]
        recv(f"y{j}", block, to_y(j))
        send(f"xp{j}", block, block, to_x(1))
        send(f"xm{j}", block, block, to_x(-1))

    def forward_x(j):
        low, high = wt.at[gat(-1, j)], wt.at[gat(1, j)]
        recv(f"xp{j}", low, to_x(-1))
        send(f"fp{j}", low.at[pl.ds(0, CUT)], low.at[pl.ds(0, CUT)], to_x(1))
        recv(f"xm{j}", high, to_x(1))
        send(f"fm{j}", high.at[pl.ds(CUT, 2 * F - CUT)], high.at[pl.ds(CUT, 2 * F - CUT)], to_x(-1))

    def finish_x(j):
        far = wt.at[gat(2, j)]
        recv(f"fp{j}", far.at[pl.ds(0, CUT)], to_x(-1))
        recv(f"fm{j}", far.at[pl.ds(CUT, 2 * F - CUT)], to_x(1))

    def block_of(s, dz):
        return nb.at[c, zat(dz) * H + (h if s == 0 else 1 - h)]

    def other_block_of(s, dz):
        return nb.at[1 - c, zat(dz) * H + (h if s == 0 else 1 - h)]

    def start_z(s):
        block = block_of(s, 0)
        send(f"zp{s}_1", block, block, to_z(1))
        send(f"zm{s}_1", block, block, to_z(-1))
        send(f"c{s}_0", block, block, to_c)

    def column_half(ref, at):
        return ref.at[:, pl.ds(at * (KH // 2), KH // 2)]

    def step_z(s, n):
        low, high = block_of(s, -n), block_of(s, n)
        if n < half:
            recv(f"zp{s}_{n}", low, to_z(-1))
            if n + 1 < half:
                send(f"zp{s}_{n + 1}", low, low, to_z(1))
            else:
                send(f"zp{s}_{n + 1}", column_half(low, 0), column_half(low, 0), to_z(1))
            recv(f"zm{s}_{n}", high, to_z(1))
            if n + 1 < half:
                send(f"zm{s}_{n + 1}", high, high, to_z(-1))
            else:
                send(f"zm{s}_{n + 1}", column_half(high, 1), column_half(high, 1), to_z(-1))
            send(f"c{s}_{-n}", low, low, to_c)
            send(f"c{s}_{n}", high, high, to_c)
        else:
            recv(f"zp{s}_{n}", column_half(low, 0), to_z(-1))
            recv(f"zm{s}_{n}", column_half(low, 1), to_z(1))
            send(f"c{s}_{n}", low, low, to_c)

    def sum_start(kind, red, rx):
        for k in range(1, X):
            send(f"{kind}r{k}", red.at[xat(k)], rx.at[k - 1], to_x(k))

    def sum_middle(kind, red, rx, ry_):
        for k in range(1, X):
            recv(f"{kind}r{k}", rx.at[k - 1], to_x(-k))
        ry_[0] = red[x] + rx[0] + rx[1] + rx[2]
        for j in range(1, Y):
            send(f"{kind}y{j}", ry_.at[0], ry_.at[j], to_y(j))

    def sum_spread(kind, red, rx, ry_):
        for j in range(1, Y):
            recv(f"{kind}y{j}", ry_.at[j], to_y(j))
        rx[X - 1] = ry_[0] + ry_[1] + ry_[2] + ry_[3]
        for k in range(1, X):
            send(f"{kind}a{k}", rx.at[X - 1], ry_.at[Y + k - 1], to_x(k))

    def sum_end(kind, red, rx, ry_):
        whole[x] = rx[X - 1]
        for k in range(1, X):
            recv(f"{kind}a{k}", ry_.at[Y + k - 1], to_x(-k))
            whole[xat(-k)] = ry_[Y + k - 1]
        return whole[...].reshape(red.shape[0] * red.shape[1], LANES)[:F]

    recv("e", pair.at[1 - c], to_c)
    nb[c, z * H + h] = pair[...].reshape(2 * T8, KH).astype(bf16)
    own = block_of(0, 0)
    start_z(0)
    send("hx", own, own, to_h)

    head_own[...] = jnp.zeros_like(head_own)
    head_own[0:B, :] = head[:, pl.ds(pl.multiple_of(grp * RB, RB), RB)].astype(f32)
    head_block = head_own[...].astype(bf16)
    w_down = dequantize(dc, 16).astype(bf16)
    product = nt(w_down, head_block)
    rows = mred.shape[0] * mred.shape[1]
    tail = jnp.zeros((rows - F, LANES), f32)
    mred[...] = jnp.concatenate([product, tail], axis=0).reshape(mred.shape)
    sum_start("m", mred, mrx)

    own_logit[...] = jnp.zeros_like(own_logit)
    own_logit[:, 0:B] = nt(hid[...], head[...])
    teach_pad[...] = jnp.zeros_like(teach_pad)
    teach_pad[0:B, :] = teach[...]
    teach_rows[...] = teach_pad[...].T.reshape(teach_rows.shape)

    step_z(0, 1)
    forward_x(0)
    spread_y(1)
    recv("hx", block_of(1, 0), to_h)
    start_z(1)
    step_z(0, 2)
    sum_middle("m", mred, mrx, mry)
    step_z(1, 1)
    forward_x(1)
    spread_y(2)
    step_z(0, 3)
    step_z(1, 2)
    sum_spread("m", mred, mrx, mry)
    finish_x(0)
    forward_x(2)
    spread_y(3)
    for n in range(4, half + 1):
        step_z(0, n)
        step_z(1, n - 1)
        if n == 5:
            forward_x(3)
    step_z(1, half)
    big_m = sum_end("m", mred, mrx, mry)
    for j in range(1, Y):
        finish_x(j)
    for s in range(2):
        for k in range(-half + 1, half + 1):
            recv(f"c{s}_{k}", other_block_of(s, k), to_c)

    tokens = acc.shape[1]
    per = X * Y // 2

    def normed_columns(g):
        at = lax.rem(g, per)
        return nb[lax.div(g, per), :, :, pl.ds(pl.multiple_of(at * RB, RB), RB)].reshape(tokens, RB)

    acc[...] = jnp.zeros_like(acc)

    def add_block(g, carry):
        acc[...] += nt(wt[g], normed_columns(g))
        return carry

    lax.fori_loop(0, X * Y, add_block, 0)
    gate, up = acc[0:F, :], acc[F : 2 * F, :]
    sig = jax.nn.sigmoid(gate)
    units = (gate * sig * up).astype(bf16)
    units_s[...] = units.astype(f32)

    m_high, m_low = split(big_m)
    share = (tn(units, m_high) + tn(units, m_low)).reshape(Z * H, C, T8, LANES)
    part[0] = share[:, 0].reshape(Z, H, T8, LANES)
    part[1] = share[:, 1].reshape(Z, H, T8, LANES)
    send("l1", part.at[1 - c], l1_in, to_c)
    recv("l1", l1_in, to_c)
    summed[...] = part[c] + l1_in[...]
    for k in range(1, Z):
        send(f"l2_{k}", summed.at[zat(k)], l2_in.at[k - 1], to_z(k))
    total = summed[z]
    for k in range(1, Z):
        recv(f"l2_{k}", l2_in.at[k - 1], to_z(-k))
        total = total + l2_in[k - 1]
    l3_out[...] = total
    l3_out[h] = l3_out[h] + own_logit[...]
    send("l3", l3_out, l3_in, to_h)
    recv("l3", l3_in, to_h)
    logits = (l3_out[...] + l3_in[...]).reshape(H * T8, LANES)

    lane = lax.broadcasted_iota(jnp.int32, (H * T8, LANES), 1)
    sub = lax.broadcasted_iota(jnp.int32, (H * T8, LANES), 0)
    valid = lane < B
    first = (z * H * C + c) * T8
    wanted = jnp.zeros((H * T8, LANES), jnp.int32)
    for at in range(H * T8):
        value = targ[first + (at // T8) * C * T8 + at % T8]
        wanted = jnp.where(sub == at, value, wanted)
    onehot = jnp.where(lane == wanted, 1.0, 0.0)

    def log_softmax(values):
        top = jnp.max(jnp.where(valid, values, -jnp.inf), axis=1, keepdims=True)
        shifted = jnp.where(valid, values - top, 0.0)
        bottom = jnp.sum(jnp.where(valid, jnp.exp(shifted), 0.0), axis=1, keepdims=True)
        return shifted - jnp.log(bottom)

    teacher = jnp.concatenate([teach_rows[z * H * C + k * C + c] for k in range(H)], axis=0)
    log_student, log_teacher = log_softmax(logits), log_softmax(teacher)
    p_student, p_teacher = jnp.exp(log_student), jnp.exp(log_teacher)
    terms = jnp.where(valid, p_teacher * (log_teacher - log_student) - onehot * log_student, 0.0)
    loss = jnp.sum(terms, axis=1, keepdims=True)
    d_own = jnp.where(valid, loss_scale * (2.0 * p_student - onehot - p_teacher), 0.0)
    dl[c, z] = d_own.reshape(H, T8, LANES)
    for k in range(1, Z):
        send(f"l4_{k}", dl.at[c, z], dl.at[c, z], to_z(k))
    loss_s[...] = jnp.broadcast_to(loss, (H * T8, LANES)).reshape(H, T8, LANES)
    loss_rows = jnp.concatenate([loss_s[h], jnp.zeros((LANES - T8, LANES), f32)], axis=0)
    loss_o[...] = loss_rows.T[0:1, 0:T8]
    for k in range(1, Z):
        recv(f"l4_{k}", dl.at[c, zat(-k)], to_z(-k))
    send("l5", dl.at[c], dl.at[c], to_c)
    recv("l5", dl.at[1 - c], to_c)
    d_logits = jnp.concatenate(
        [dl[0].reshape(Z * H, 1, T8, LANES), dl[1].reshape(Z * H, 1, T8, LANES)], axis=1
    ).reshape(tokens, LANES)

    d_high, d_low = split(d_logits)
    d_units = nt(m_high, d_high) + nt(m_high, d_low) + nt(m_low, d_high)
    gate, up = acc[0:F, :], acc[F : 2 * F, :]
    sig = jax.nn.sigmoid(gate)
    d_gate = d_units * up * sig * (1.0 + gate * (1.0 - sig))
    d_up = d_units * (gate * sig)
    units = units_s[...].astype(bf16)
    product = nn(units, d_high) + nn(units, d_low)
    nred[...] = jnp.concatenate([product, tail], axis=0).reshape(nred.shape)
    sum_start("n", nred, nrx)
    acc[0:F, :] = d_gate
    acc[F : 2 * F, :] = d_up
    d_both = acc[...].astype(bf16)

    order = (2, 3, 1, 0)

    def partial(dx, j):
        g = gat(dx, j)
        grads[(dx % X) * Y + j] = nn(d_both, normed_columns(g)).astype(bf16)

    def slot(dx, j):
        return (dx % X) * Y + j

    for j in order:
        partial(2, j)
        far = grads.at[slot(2, j)]
        send(f"ra{j}", far.at[pl.ds(0, CUT)], ra.at[j], to_x(1))
        send(f"rb{j}", far.at[pl.ds(CUT, 2 * F - CUT)], rb.at[j], to_x(-1))
        partial(1, j)
        partial(-1, j)
        partial(0, j)
    sum_middle("n", nred, nrx, nry)
    for j in order:
        recv(f"ra{j}", ra.at[j], to_x(-1))
        at = slot(1, j)
        joined = grads[at, 0:CUT, :].astype(f32) + ra[j].astype(f32)
        grads[at, 0:CUT, :] = joined.astype(bf16)
        send(f"sp{j}", grads.at[at], sp.at[j], to_x(1))
        recv(f"rb{j}", rb.at[j], to_x(1))
        at = slot(-1, j)
        joined = grads[at, CUT : 2 * F, :].astype(f32) + rb[j].astype(f32)
        grads[at, CUT : 2 * F, :] = joined.astype(bf16)
        send(f"sm{j}", grads.at[at], sm.at[j], to_x(-1))
    sum_spread("n", nred, nrx, nry)
    big_n = None
    for j in order:
        if j == 0:
            big_n = sum_end("n", nred, nrx, nry)
            n_high, n_low = split(big_n)
            gd_o[...] = nn(n_high, head_own[...].astype(bf16)) + nn(n_low, head_own[...].astype(bf16))
        recv(f"sp{j}", sp.at[j], to_x(-1))
        recv(f"sm{j}", sm.at[j], to_x(1))
        at = slot(0, j)
        total = grads[at].astype(f32) + sp[j].astype(f32) + sm[j].astype(f32)
        if j:
            grads[at] = total.astype(bf16)
            send(f"ry{j}", grads.at[at], ry.at[j - 1], to_y(j))
        else:
            acc[:, 0:RB] = total
    for j in (2, 3, 1):
        recv(f"ry{j}", ry.at[j - 1], to_y(j))
    result = acc[:, 0:RB] + ry[0].astype(f32) + ry[1].astype(f32) + ry[2].astype(f32)
    gg_o[...] = result[0:F]
    gu_o[...] = result[F : 2 * F]
    wires.finish()


def solution(mesh):
    Z = mesh.shape["shard"] // (H * C)
    names = wire_names(Z)

    def local(hidden, norm_gain, gate_codes, gate_scales, up_codes, up_scales, down_codes, down_scales, head, teacher, targets):
        T8, D = hidden.shape
        RB, F = gate_codes.shape
        B = head.shape[1]
        tokens = teacher.shape[0]
        KH = D // 2
        chunk = -(-F // (8 * X)) * 8
        vmem = pl.BlockSpec(memory_space=pltpu.VMEM)
        smem = pl.BlockSpec(memory_space=pltpu.SMEM)
        grad = jax.ShapeDtypeStruct((F, RB), f32)
        V = pltpu.VMEM
        scratch = [
            V((2, T8, KH), f32),
            V((2, T8, KH), f32),
            V((2, Z * H, 2 * T8, KH), bf16),
            V((X * Y, 2 * F, RB), bf16),
            V((128, 256), f32),
            V((LANES, RB), f32),
            V((T8, LANES), f32),
            V((LANES, tokens), f32),
            V((tokens // T8, T8, LANES), f32),
            V((2 * F, tokens), f32),
            V((F, tokens), f32),
            V((X, chunk, LANES), f32),
            V((X, chunk, LANES), f32),
            V((X, chunk, LANES), f32),
            V((X + Y, chunk, LANES), f32),
            V((X, chunk, LANES), f32),
            V((X, chunk, LANES), f32),
            V((X + Y, chunk, LANES), f32),
            V((C, Z, H, T8, LANES), f32),
            V((Z, H, T8, LANES), f32),
            V((Z, H, T8, LANES), f32),
            V((Z - 1, H, T8, LANES), f32),
            V((H, T8, LANES), f32),
            V((H, T8, LANES), f32),
            V((C, Z, H, T8, LANES), f32),
            V((H, T8, LANES), f32),
            V((X * Y, 2 * F, RB), bf16),
            V((Y, CUT, RB), bf16),
            V((Y, 2 * F - CUT, RB), bf16),
            V((Y, 2 * F, RB), bf16),
            V((Y, 2 * F, RB), bf16),
            V((Y - 1, 2 * F, RB), bf16),
            pltpu.SemaphoreType.DMA((len(names),)),
            pltpu.SemaphoreType.DMA((len(names),)),
        ]
        loss, gate, up, down = pl.pallas_call(
            functools.partial(kernel, names, Z, D, F, B),
            out_shape=(jax.ShapeDtypeStruct((1, T8), f32), grad, grad, grad),
            in_specs=[vmem] * 10 + [smem],
            out_specs=(vmem,) * 4,
            scratch_shapes=scratch,
            compiler_params=pltpu.CompilerParams(
                collective_id=0, has_side_effects=True, vmem_limit_bytes=50 << 20
            ),
            name="step",
        )(
            hidden, norm_gain.reshape(1, D), gate_codes.T, gate_scales, up_codes.T, up_scales,
            down_codes.T, down_scales, head.T, teacher.T, targets,
        )
        return (loss.reshape(T8), gate.T, up.T, down.T)

    in_specs = (
        P(("grp", "shard"), None),
        P(),
        P("grp", "shard"),
        P("grp", "shard"),
        P("grp", "shard"),
        P("grp", "shard"),
        P("grp", "shard"),
        P("grp", "shard"),
        P(),
        P("grp", None),
        P("grp"),
    )
    out_specs = (P(("grp", "shard")), P("grp", "shard"), P("grp", "shard"), P("grp", "shard"))
    return jax.shard_map(local, mesh=mesh, in_specs=in_specs, out_specs=out_specs, check_vma=False)
```

time: 989 us -> 124 us (0.13)
  waiting for transfers between devices: 925 us -> 0 us
  Pallas kernels: 0 us -> 113 us
  matrix products: 20.1 us -> 0 us
  between operations: 14.3 us -> 0.69 us
  other arithmetic: 11.4 us -> 0 us
    psum x1 -> x0, waiting for transfers between devices: 477 us -> none  [local(): logits = lax.psum(partial_value, 'shard')]
    all_gather x4 -> x0, waiting for transfers between devices: 356 us -> none  [the longest x1 143 us: local(): gathered = lax.all_gather(normed, 'shard', axis=0, tiled=True)]
    pallas_call x0 -> x1, Pallas kernels: none -> 113 us  [local(): pl.pallas_call(functools.partial(kernel, names, Z, D, F, B), out_shape=(j...]
    reduce_scatter x1 -> x0, waiting for transfers between devices: 91.5 us -> none  [local(): lax.psum_scatter(jnp.concatenate([weight_term(gathered, d_gate), weight_t...]
    dot_general x10 -> x0, matrix products: 20.1 us -> none  [the longest x1 3.86 us: local(): jnp.dot(d_logits, head_float.T, precision=lax.Precision.HIGHEST)]
  transfers between devices with their start and end apart: 6 -> 0, of which waited for: 6 -> 0; matrix products, arithmetic and copies ran while one was open for 2% -> 0% of each run, Pallas kernels for 0% -> 0%
where the time goes in v1:
time: 124 us; the launch traced here: 123 us
  Pallas kernels  113 us (91%)
  local copies, waits for them, and re-layouts  9.48 us (8%)
    pallas_call x1, Pallas kernels, local(): pl.pallas_call(functools.partial(kernel, names, Z, D, F, B), out_shape=(j...  113 us
    unnamed x26, local copies, waits for them, and re-layouts  9.48 us

profile of v1, /device:TPU:1, one launch (start us, length us, event | category | flops | bytes accessed | tf_op | source)
XLA Modules:
  0.0 123.2 jit_solution(6619364135138097212)
XLA Ops:
  0.6 0.0 copy-start.10
  0.6 0.0 copy-start.9
  0.7 0.0 copy-start.8
  0.7 0.0 copy-start.7
  0.7 0.6 copy-done.10
  1.3 0.0 copy-done.9
  1.3 0.0 copy-done.8
  1.3 0.0 copy-done.7
  1.4 0.0 copy-start
  1.4 1.2 copy-done
  2.5 0.0 copy-start.1
  2.5 0.9 copy-done.1
  3.4 0.0 copy-start.2
  3.4 0.9 copy-done.2
  4.3 0.0 copy-start.3
  4.3 0.9 copy-done.3
  5.2 0.0 copy-start.4
  5.2 0.9 copy-done.4
  6.1 0.0 copy-start.5
  6.1 0.8 copy-done.5
  6.9 0.0 copy-start.6
  6.9 0.7 copy-done.6
  7.7 113.1 %step.1 = (f32[1,8]{1,0:T(1,128)S(1)}, f32[152,256]{1,0:T(8,128)S(1)}, f32[152,256]{1,0:T(8,128)S(1)}, f32[152,256]{1,0:T(8,128)S(1)}) custom-call(bf16[8,4096]{1,0:T(8,128)(2,1)S(1)} %copy-done.5, f32[1,4096]{1,0:T(1,128)S(1)} %bitcast.18, bf16[152,256]{1,0:T(8,128)(2,1)S(1)} %bitcast.15, f32[2,152]{1,0:T(2,128)S(1)} %copy-done.7, ...), custom_call_target="tpu_custom_call" | custom-call | tf_op jit(solution)/shard_map/step/pallas_call | solution.py:491
  120.7 0.5 copy.19
  121.2 0.7 copy.20
  121.9 0.7 copy.21
  122.6 0.7 copy.22
Async XLA Ops:
  0.6 0.7 copy-start.10
  0.6 0.7 copy-start.9
  0.7 0.7 copy-start.8
  0.7 0.7 copy-start.7
  1.4 1.2 copy-start
  2.5 0.9 copy-start.1
  3.4 0.9 copy-start.2
  4.3 0.9 copy-start.3
  5.2 0.9 copy-start.4
  6.1 0.8 copy-start.5
  6.9 0.7 copy-start.6

commit v2 on v1

v2 whole, which is shorter than its diff:
```python
import functools

import jax
import jax.numpy as jnp
from jax import lax
from jax.experimental import pallas as pl
from jax.experimental.pallas import tpu as pltpu
from jax.sharding import PartitionSpec as P

eps = 1e-05
loss_scale = 64.0
MESH = pl.DeviceIdType.MESH
f32, bf16 = jnp.float32, jnp.bfloat16

X, Y = 4, 4
H, C = 2, 2
CUT = 160
LANES = 128


def nt(left, right):
    return lax.dot_general(left, right, (((1,), (1,)), ((), ())), preferred_element_type=f32)


def nn(left, right):
    return jnp.dot(left, right, preferred_element_type=f32)


def tn(left, right):
    return lax.dot_general(left, right, (((0,), (0,)), ((), ())), preferred_element_type=f32)


def split(value):
    high = value.astype(bf16)
    return high, (value - high.astype(f32)).astype(bf16)


class Wires:
    def __init__(self, send_sems, recv_sems, names):
        self.send_sems, self.recv_sems, self.names, self.started = send_sems, recv_sems, names, []

    def slot(self, name):
        return self.names[name]

    def describe(self, name, src, dst, device):
        at = self.slot(name)
        return pltpu.make_async_remote_copy(
            src_ref=src,
            dst_ref=dst,
            send_sem=self.send_sems.at[at],
            recv_sem=self.recv_sems.at[at],
            device_id=device,
            device_id_type=MESH,
        )

    def send(self, name, src, dst, device):
        copy = self.describe(name, src, dst, device)
        copy.start()
        self.started.append(copy)

    def recv(self, name, dst, device):
        self.describe(name, dst, dst, device).wait_recv()

    def finish(self):
        for copy in self.started:
            copy.wait_send()


def wire_names(Z):
    half = Z // 2
    names = ["e", "hx0", "hx1", "l1", "l3", "l5"]
    for j in range(Y):
        names += [f"{kind}{j}" for kind in ("fp", "fm", "ra", "rb", "sp", "sm", "ry")]
        names += [f"{kind}{p}{j}" for kind in ("y", "xp", "xm") for p in "AB"]
    for s in range(2):
        for n in range(1, half + 1):
            names += [f"z{way}{s}{q}_{n}" for way in "pm" for q in range(2)]
        for k in range(-half, half + 1):
            names.append(f"c{s}_{k}")
    for k in range(1, Z):
        names += [f"l2_{k}", f"l4_{k}"]
    for kind in ("m", "n"):
        for k in range(1, X):
            names += [f"{kind}r{k}", f"{kind}a{k}"]
        for j in range(1, Y):
            names.append(f"{kind}y{j}")
    return {name: at for at, name in enumerate(names)}


def kernel(
    names, Z, D, F, B,
    hid, gain, gc, gs, uc, us, dc, ds, head, teach, targ,
    loss_o, gg_o, gu_o, gd_o,
    halves, pair, nb, wt, scale_pad, head_own, own_logit, teach_pad, teach_rows,
    acc, units_s, whole, mred, mrx, mry, nred, nrx, nry,
    part, l1_in, summed, l2_in, l3_out, l3_in, dl, loss_s,
    grads, ra, rb, sp, sm, ry,
    send_sems, recv_sems,
):
    grp, sh = lax.axis_index("grp"), lax.axis_index("shard")
    x, y = lax.div(grp, Y), lax.rem(grp, Y)
    z, h, c = lax.div(sh, H * C), lax.rem(lax.div(sh, C), H), lax.rem(sh, C)
    half = Z // 2
    RB = D // (X * Y)
    T8 = hid.shape[0]
    KH = D // 2

    def xat(dx):
        return lax.rem(x + dx % X, X) if dx % X else x

    def yat(j):
        return (y, y + 1 - 2 * lax.rem(y, 2), y + 2 - 4 * lax.div(y, 2), 3 - y)[j]

    def zat(dz):
        return lax.rem(z + dz % Z, Z) if dz % Z else z

    def to_x(dx):
        return {"grp": xat(dx) * Y + y}

    def to_y(j):
        return {"grp": x * Y + yat(j)}

    def hat(flip):
        return 1 - h if flip else h

    def to_z(dz, flip=0):
        return {"shard": (zat(dz) * H + hat(flip)) * C + c}

    to_h = to_z(0, 1)
    to_c = {"shard": (z * H + h) * C + (1 - c)}

    wires = Wires(send_sems, recv_sems, names)
    send, recv = wires.send, wires.recv

    barrier = pltpu.get_barrier_semaphore()
    around = sorted(range(1, Z), key=lambda k: -min(k, Z - k))
    peers = [to_z(k) for k in around] + [to_h]
    peers += [to_y(j) for j in range(1, Y)] + [to_x(k) for k in range(1, X)] + [to_c]
    for peer in peers:
        pl.semaphore_signal(barrier, inc=1, device_id=peer, device_id_type=MESH)

    xf = hid[...].astype(f32)
    mean = jnp.mean(xf * xf, axis=1, keepdims=True)
    normed = (xf * lax.rsqrt(mean + eps) * gain[...]).astype(bf16).astype(f32)
    halves[0] = normed[:, :KH]
    halves[1] = normed[:, KH:]
    pair[c] = halves[c]

    scale_pad[...] = jnp.zeros_like(scale_pad)
    scale_pad[0:2, 0:F] = gs[...]
    scale_pad[8:10, 0:F] = us[...]
    scale_pad[16:18, 0:F] = ds[...]
    columns = scale_pad[...].T

    def dequantize(codes, at):
        value = codes[...].astype(f32)
        mid = RB // 2
        left = value[:, :mid] * columns[:F, at : at + 1]
        right = value[:, mid:] * columns[:F, at + 1 : at + 2]
        return jnp.concatenate([left, right], axis=1)

    wt[grp] = jnp.concatenate([dequantize(gc, 0), dequantize(uc, 8)], axis=0).astype(bf16)

    head_own[...] = jnp.zeros_like(head_own)
    head_own[0:B, :] = head[:, pl.ds(pl.multiple_of(grp * RB, RB), RB)].astype(f32)
    head_block = head_own[...].astype(bf16)
    w_down = dequantize(dc, 16).astype(bf16)
    product = nt(w_down, head_block)
    rows = mred.shape[0] * mred.shape[1]
    tail = jnp.zeros((rows - F, LANES), f32)
    mred[...] = jnp.concatenate([product, tail], axis=0).reshape(mred.shape)

    pl.semaphore_wait(barrier, len(peers))

    send("e", halves.at[1 - c], pair.at[c], to_c)
    def gat(dx, j):
        return xat(dx) * Y + yat(j)

    def rows_of(block, p):
        return block.at[pl.ds(0, CUT)] if p == "A" else block.at[pl.ds(CUT, 2 * F - CUT)]

    def pass_on(name, block, device):
        send(name, block, block, device)

    def spread_x(j):
        block = wt.at[gat(0, j)]
        if j:
            recv(f"yA{j}", rows_of(block, "A"), to_y(j))
        if j == 2:
            pass_on("yA3", rows_of(block, "A"), to_y(1))
        pass_on(f"xpA{j}", rows_of(block, "A"), to_x(1))
        if j:
            recv(f"yB{j}", rows_of(block, "B"), to_y(j))
        if j == 2:
            pass_on("yB3", rows_of(block, "B"), to_y(1))
        pass_on(f"xmB{j}", rows_of(block, "B"), to_x(-1))
        pass_on(f"xpB{j}", rows_of(block, "B"), to_x(1))
        pass_on(f"xmA{j}", rows_of(block, "A"), to_x(-1))

    def forward_x(j):
        low, high = rows_of(wt.at[gat(-1, j)], "A"), rows_of(wt.at[gat(1, j)], "B")
        recv(f"xpA{j}", low, to_x(-1))
        pass_on(f"fp{j}", low, to_x(1))
        recv(f"xmB{j}", high, to_x(1))
        pass_on(f"fm{j}", high, to_x(-1))

    def finish_x(j):
        recv(f"xpB{j}", rows_of(wt.at[gat(-1, j)], "B"), to_x(-1))
        recv(f"xmA{j}", rows_of(wt.at[gat(1, j)], "A"), to_x(1))
        opposite = wt.at[gat(2, j)]
        recv(f"fp{j}", rows_of(opposite, "A"), to_x(-1))
        recv(f"fm{j}", rows_of(opposite, "B"), to_x(1))

    def start_y(p, j):
        pass_on(f"y{p}{j}", rows_of(wt.at[grp], p), to_y(j))

    def block_of(s, dz):
        return nb.at[c, zat(dz) * H + (h if s == 0 else 1 - h)]

    def other_block_of(s, dz):
        return nb.at[1 - c, zat(dz) * H + (h if s == 0 else 1 - h)]

    def column_half(ref, at):
        return ref.at[:, pl.ds(at * (KH // 2), KH // 2)]

    def start_z(s):
        block = block_of(s, 0)
        for q in range(2):
            if s:
                recv(f"hx{q}", column_half(block, q), to_h)
            pass_on(f"zp{s}{q}_1", column_half(block, q), to_z(1))
            pass_on(f"zm{s}{q}_1", column_half(block, q), to_z(-1))
        pass_on(f"c{s}_0", block, to_c)

    def step_z(s, n):
        low, high = block_of(s, -n), block_of(s, n)
        for q in range(2):
            if n < half:
                recv(f"zp{s}{q}_{n}", column_half(low, q), to_z(-1))
                if n + 1 < half or q == 0:
                    pass_on(f"zp{s}{q}_{n + 1}", column_half(low, q), to_z(1))
                recv(f"zm{s}{q}_{n}", column_half(high, q), to_z(1))
                if n + 1 < half or q == 1:
                    pass_on(f"zm{s}{q}_{n + 1}", column_half(high, q), to_z(-1))
            elif q == 0:
                recv(f"zp{s}0_{n}", column_half(low, 0), to_z(-1))
            else:
                recv(f"zm{s}1_{n}", column_half(low, 1), to_z(1))
        if n < half:
            pass_on(f"c{s}_{-n}", low, to_c)
        pass_on(f"c{s}_{n}", high, to_c)

    def sum_start(kind, red, rx):
        for k in range(1, X):
            send(f"{kind}r{k}", red.at[xat(k)], rx.at[k - 1], to_x(k))

    def sum_middle(kind, red, rx, ry_):
        for k in range(1, X):
            recv(f"{kind}r{k}", rx.at[k - 1], to_x(-k))
        ry_[0] = red[x] + rx[0] + rx[1] + rx[2]
        for j in range(1, Y):
            send(f"{kind}y{j}", ry_.at[0], ry_.at[j], to_y(j))

    def sum_spread(kind, red, rx, ry_):
        for j in range(1, Y):
            recv(f"{kind}y{j}", ry_.at[j], to_y(j))
        rx[X - 1] = ry_[0] + ry_[1] + ry_[2] + ry_[3]
        for k in range(1, X):
            send(f"{kind}a{k}", rx.at[X - 1], ry_.at[Y + k - 1], to_x(k))

    def sum_end(kind, red, rx, ry_):
        whole[x] = rx[X - 1]
        for k in range(1, X):
            recv(f"{kind}a{k}", ry_.at[Y + k - 1], to_x(-k))
            whole[xat(-k)] = ry_[Y + k - 1]
        return whole[...].reshape(red.shape[0] * red.shape[1], LANES)[:F]

    sum_start("m", mred, mrx)
    spread_x(0)
    start_y("A", 1)
    recv("e", pair.at[1 - c], to_c)
    nb[c, z * H + h] = pair[...].reshape(2 * T8, KH).astype(bf16)
    own = block_of(0, 0)
    for q in range(2):
        pass_on(f"hx{q}", column_half(own, q), to_h)
    start_z(0)
    start_y("B", 1)
    start_y("A", 2)
    start_y("B", 2)

    step_z(0, 1)
    forward_x(0)
    step_z(0, 2)
    start_z(1)
    spread_x(1)
    step_z(0, 3)
    step_z(1, 1)
    spread_x(2)
    step_z(0, 4)
    step_z(1, 2)
    forward_x(1)
    sum_middle("m", mred, mrx, mry)
    step_z(0, 5)
    step_z(1, 3)
    spread_x(3)
    forward_x(2)
    step_z(0, 6)
    step_z(1, 4)
    forward_x(3)
    sum_spread("m", mred, mrx, mry)
    step_z(1, 5)
    step_z(1, 6)
    for j in range(Y):
        finish_x(j)
    for s in range(2):
        for k in range(-half + 1, half + 1):
            recv(f"c{s}_{k}", other_block_of(s, k), to_c)

    tokens = acc.shape[1]
    per = X * Y // 2

    def normed_columns(g):
        at = lax.rem(g, per)
        return nb[lax.div(g, per), :, :, pl.ds(pl.multiple_of(at * RB, RB), RB)].reshape(tokens, RB)

    def add_blocks(at, carry):
        total = acc[...]
        for k in range(4):
            total = total + nt(wt[4 * at + k], normed_columns(4 * at + k))
        acc[...] = total
        return carry

    acc[...] = jnp.zeros_like(acc)
    lax.fori_loop(0, X * Y // 4, add_blocks, 0)
    gate, up = acc[0:F, :], acc[F : 2 * F, :]
    sig = jax.nn.sigmoid(gate)
    units = (gate * sig * up).astype(bf16)
    units_s[...] = units.astype(f32)

    big_m = sum_end("m", mred, mrx, mry)
    m_high, m_low = split(big_m)
    share = (tn(units, m_high) + tn(units, m_low)).reshape(Z * H, C, T8, LANES)
    part[0] = share[:, 0].reshape(Z, H, T8, LANES)
    part[1] = share[:, 1].reshape(Z, H, T8, LANES)
    send("l1", part.at[1 - c], l1_in, to_c)
    recv("l1", l1_in, to_c)
    summed[...] = part[c] + l1_in[...]
    for k in around:
        send(f"l2_{k}", summed.at[zat(k)], l2_in.at[k], to_z(k))

    own_logit[...] = jnp.zeros_like(own_logit)
    own_logit[:, 0:B] = nt(hid[...], head[...])
    teach_pad[...] = jnp.zeros_like(teach_pad)
    teach_pad[0:B, :] = teach[...]
    teach_rows[...] = teach_pad[...].T.reshape(teach_rows.shape)
    lane = lax.broadcasted_iota(jnp.int32, (H * T8, LANES), 1)
    sub = lax.broadcasted_iota(jnp.int32, (H * T8, LANES), 0)
    valid = lane < B
    first = (z * H * C + c) * T8
    wanted = jnp.zeros((H * T8, LANES), jnp.int32)
    for at in range(H * T8):
        value = targ[first + (at // T8) * C * T8 + at % T8]
        wanted = jnp.where(sub == at, value, wanted)
    onehot = jnp.where(lane == wanted, 1.0, 0.0)

    def log_softmax(values):
        top = jnp.max(jnp.where(valid, values, -jnp.inf), axis=1, keepdims=True)
        shifted = jnp.where(valid, values - top, 0.0)
        bottom = jnp.sum(jnp.where(valid, jnp.exp(shifted), 0.0), axis=1, keepdims=True)
        return shifted - jnp.log(bottom)

    teacher = jnp.concatenate([teach_rows[z * H * C + k * C + c] for k in range(H)], axis=0)
    log_teacher = log_softmax(teacher)
    p_teacher = jnp.exp(log_teacher)

    total = summed[z]
    for k in reversed(around):
        recv(f"l2_{k}", l2_in.at[k], to_z(-k))
        total = total + l2_in[k]
    l3_out[...] = total
    l3_out[h] = l3_out[h] + own_logit[...]
    send("l3", l3_out, l3_in, to_h)
    acc[0:F, :] = up * sig * (1.0 + gate * (1.0 - sig))
    acc[F : 2 * F, :] = gate * sig
    recv("l3", l3_in, to_h)
    logits = (l3_out[...] + l3_in[...]).reshape(H * T8, LANES)

    log_student = log_softmax(logits)
    p_student = jnp.exp(log_student)
    d_own = jnp.where(valid, loss_scale * (2.0 * p_student - onehot - p_teacher), 0.0)
    dl[c, z] = d_own.astype(bf16)
    for k in around:
        pass_on(f"l4_{k}", dl.at[c, z], to_z(k))
    terms = jnp.where(valid, p_teacher * (log_teacher - log_student) - onehot * log_student, 0.0)
    loss = jnp.broadcast_to(jnp.sum(terms, axis=1, keepdims=True), (H * T8, LANES))
    loss_s[...] = loss.reshape(H, T8, LANES)
    loss_rows = jnp.concatenate([loss_s[h], jnp.zeros((LANES - T8, LANES), f32)], axis=0)
    loss_o[...] = loss_rows.T[0:1, 0:T8]
    for k in reversed(around):
        recv(f"l4_{k}", dl.at[c, zat(-k)], to_z(-k))
    pass_on("l5", dl.at[c], to_c)
    recv("l5", dl.at[1 - c], to_c)
    d_logits = jnp.concatenate(
        [dl[k].astype(f32).reshape(Z * H, 1, T8, LANES) for k in range(C)], axis=1
    ).reshape(tokens, LANES)

    d_logits = d_logits.astype(bf16)
    d_units = nt(m_high, d_logits) + nt(m_low, d_logits)
    acc[0:F, :] = d_units * acc[0:F, :]
    acc[F : 2 * F, :] = d_units * acc[F : 2 * F, :]
    d_both = acc[...].astype(bf16)


    def partial(dx, j):
        g = gat(dx, j)
        grads[(dx % X) * Y + j] = nn(d_both, normed_columns(g)).astype(bf16)

    def slot(dx, j):
        return (dx % X) * Y + j

    def start_rs(j):
        partial(2, j)
        opposite = grads.at[slot(2, j)]
        send(f"ra{j}", rows_of(opposite, "A"), ra.at[j], to_x(1))
        send(f"rb{j}", rows_of(opposite, "B"), rb.at[j], to_x(-1))

    def join_rs(j):
        partial(1, j)
        recv(f"ra{j}", ra.at[j], to_x(-1))
        at = slot(1, j)
        joined = grads[at, 0:CUT, :].astype(f32) + ra[j].astype(f32)
        grads[at, 0:CUT, :] = joined.astype(bf16)
        send(f"sp{j}", grads.at[at], sp.at[j], to_x(1))
        partial(-1, j)
        recv(f"rb{j}", rb.at[j], to_x(1))
        at = slot(-1, j)
        joined = grads[at, CUT : 2 * F, :].astype(f32) + rb[j].astype(f32)
        grads[at, CUT : 2 * F, :] = joined.astype(bf16)
        send(f"sm{j}", grads.at[at], sm.at[j], to_x(-1))
        partial(0, j)

    def finish_rs(j):
        recv(f"sp{j}", sp.at[j], to_x(-1))
        recv(f"sm{j}", sm.at[j], to_x(1))
        at = slot(0, j)
        total = grads[at].astype(f32) + sp[j].astype(f32) + sm[j].astype(f32)
        if j == 2:
            recv("ry3", ry.at[2], to_y(1))
            total = total + ry[2].astype(f32)
        if j == 0:
            return total
        grads[at] = total.astype(bf16)
        send(f"ry{j}", grads.at[at], ry.at[j - 1], to_y(2 if j == 2 else 1))

    start_rs(3)
    product = nn(units_s[...].astype(bf16), d_logits)
    nred[...] = jnp.concatenate([product, tail], axis=0).reshape(nred.shape)
    sum_start("n", nred, nrx)
    start_rs(2)
    join_rs(3)
    start_rs(1)
    join_rs(2)
    start_rs(0)
    finish_rs(3)
    sum_middle("n", nred, nrx, nry)
    join_rs(1)
    finish_rs(2)
    sum_spread("n", nred, nrx, nry)
    join_rs(0)
    finish_rs(1)
    n_high, n_low = split(sum_end("n", nred, nrx, nry))
    head_block = head_own[...].astype(bf16)
    gd_o[...] = nn(n_high, head_block) + nn(n_low, head_block)
    result = finish_rs(0)
    for j in (1, 2):
        recv(f"ry{j}", ry.at[j - 1], to_y(j))
        result = result + ry[j - 1].astype(f32)
    gg_o[...] = result[0:F]
    gu_o[...] = result[F : 2 * F]
    wires.finish()


def solution(mesh):
    Z = mesh.shape["shard"] // (H * C)
    names = wire_names(Z)

    def local(hidden, norm_gain, gate_codes, gate_scales, up_codes, up_scales, down_codes, down_scales, head, teacher, targets):
        T8, D = hidden.shape
        RB, F = gate_codes.shape
        B = head.shape[1]
        tokens = teacher.shape[0]
        KH = D // 2
        chunk = -(-F // (8 * X)) * 8
        vmem = pl.BlockSpec(memory_space=pltpu.VMEM)
        smem = pl.BlockSpec(memory_space=pltpu.SMEM)
        grad = jax.ShapeDtypeStruct((F, RB), f32)
        V = pltpu.VMEM
        scratch = [
            V((2, T8, KH), f32),
            V((2, T8, KH), f32),
            V((2, Z * H, 2 * T8, KH), bf16),
            V((X * Y, 2 * F, RB), bf16),
            V((128, 256), f32),
            V((LANES, RB), f32),
            V((T8, LANES), f32),
            V((LANES, tokens), f32),
            V((tokens // T8, T8, LANES), f32),
            V((2 * F, tokens), f32),
            V((F, tokens), f32),
            V((X, chunk, LANES), f32),
            V((X, chunk, LANES), f32),
            V((X, chunk, LANES), f32),
            V((X + Y, chunk, LANES), f32),
            V((X, chunk, LANES), f32),
            V((X, chunk, LANES), f32),
            V((X + Y, chunk, LANES), f32),
            V((C, Z, H, T8, LANES), f32),
            V((Z, H, T8, LANES), f32),
            V((Z, H, T8, LANES), f32),
            V((Z, H, T8, LANES), f32),
            V((H, T8, LANES), f32),
            V((H, T8, LANES), f32),
            V((C, Z, H * T8, LANES), bf16),
            V((H, T8, LANES), f32),
            V((X * Y, 2 * F, RB), bf16),
            V((Y, CUT, RB), bf16),
            V((Y, 2 * F - CUT, RB), bf16),
            V((Y, 2 * F, RB), bf16),
            V((Y, 2 * F, RB), bf16),
            V((Y - 1, 2 * F, RB), bf16),
            pltpu.SemaphoreType.DMA((len(names),)),
            pltpu.SemaphoreType.DMA((len(names),)),
        ]
        loss, gate, up, down = pl.pallas_call(
            functools.partial(kernel, names, Z, D, F, B),
            out_shape=(jax.ShapeDtypeStruct((1, T8), f32), grad, grad, grad),
            in_specs=[pl.BlockSpec()] * 10 + [smem],
            out_specs=(vmem,) * 4,
            scratch_shapes=scratch,
            compiler_params=pltpu.CompilerParams(
                collective_id=0, has_side_effects=True, vmem_limit_bytes=62 << 20
            ),
            name="step",
        )(
            hidden, norm_gain.reshape(1, D), gate_codes.T, gate_scales, up_codes.T, up_scales,
            down_codes.T, down_scales, head.T, teacher.T, targets,
        )
        return (loss.reshape(T8), gate.T, up.T, down.T)

    in_specs = (
        P(("grp", "shard"), None),
        P(),
        P("grp", "shard"),
        P("grp", "shard"),
        P("grp", "shard"),
        P("grp", "shard"),
        P("grp", "shard"),
        P("grp", "shard"),
        P(),
        P("grp", None),
        P("grp"),
    )
    out_specs = (P(("grp", "shard")), P("grp", "shard"), P("grp", "shard"), P("grp", "shard"))
    return jax.shard_map(local, mesh=mesh, in_specs=in_specs, out_specs=out_specs, check_vma=False)
```

time: 124 us -> 111 us (0.90)
  Pallas kernels: 113 us -> 106 us
  local copies, waits for them, and re-layouts: 9.48 us -> 4.43 us
    pallas_call x1, Pallas kernels: 113 us -> 106 us  [local(): pl.pallas_call(functools.partial(kernel, names, Z, D, F, B), out_shape=(j...]
    unnamed x26 -> x10, local copies, waits for them, and re-layouts: 9.48 us -> 4.43 us
where the time goes in v2:
time: 111 us
  Pallas kernels  106 us (95%)
  local copies, waits for them, and re-layouts  4.43 us (4%)
    pallas_call x1, Pallas kernels, local(): pl.pallas_call(functools.partial(kernel, names, Z, D, F, B), out_shape=(j...  106 us
    unnamed x10, local copies, waits for them, and re-layouts  4.43 us

profile of v2, /device:TPU:1, one launch (start us, length us, event | category | flops | bytes accessed | tf_op | source)
XLA Modules:
  0.0 110.9 jit_solution(6948325674166865465)
XLA Ops:
  0.6 105.8 %step.1 = (f32[1,8]{1,0:T(1,128)}, f32[152,256]{1,0:T(8,128)}, f32[152,256]{1,0:T(8,128)}, f32[152,256]{1,0:T(8,128)}) custom-call(bf16[8,4096]{1,0:T(8,128)(2,1)} %hid.1, f32[1,4096]{1,0:T(1,128)} %bitcast.18, bf16[152,256]{1,0:T(8,128)(2,1)} %bitcast.15, f32[2,152]{1,0:T(2,128)} %gs.1, bf16[152,256]{1,0:T(8,128)(2,1)} %bitcast.16, f32[2,152]{1,0:T(2,128)} %us.1, ...), custom_call_target="tpu_custom_call" | custom-call | tf_op jit(solution)/shard_map/step/pallas_call | solution.py:534
  106.5 0.0 copy-start.2
  106.5 0.7 copy-done.2
  107.2 0.5 copy.19
  107.7 0.0 copy-start.1
  107.7 1.6 %copy.20 = f32[256,152]{0,1:T(8,128)} copy(f32[256,152]{0,1:T(8,128)} %bitcast.14) | data formatting | bytes 311296
  109.3 0.0 copy-done.1
  109.3 0.0 copy-start
  109.3 0.7 copy.21
  110.0 0.3 copy-done
  110.3 0.7 copy.22
Async XLA Ops:
  106.5 0.7 copy-start.2
  107.7 1.6 %copy-start.1 = (f32[152,256]{1,0:T(8,128)S(1)}, f32[152,256]{1,0:T(8,128)}, u32[]{:S(2)}) copy-start(f32[152,256]{1,0:T(8,128)} %get-tuple-element.10) | copy-start | bytes 466948
  109.3 1.0 copy-start

commit v3 on v2

--- a/solution.py
+++ b/solution.py
@@ -14,7 +14,9 @@
 
 X, Y = 4, 4
 H, C = 2, 2
+REACH = ((0, 1, 1, 1, 1, 1, 1), (0, 1, 1, 1, 1, 1, 0))
 CUT = 160
+CUT_1 = 240
 LANES = 128
 
 
@@ -68,9 +70,9 @@
 
 def wire_names(Z):
     half = Z // 2
-    names = ["e", "hx0", "hx1", "l1", "l3", "l5"]
+    names = ["e", "hx0", "hx1", "hy0", "hy1", "l1", "l3", "l5"]
     for j in range(Y):
-        names += [f"{kind}{j}" for kind in ("fp", "fm", "ra", "rb", "sp", "sm", "ry")]
+        names += [f"{kind}{j}" for kind in ("fp", "fm", "ra", "rb", "sp", "sm", "ry", "rq")]
         names += [f"{kind}{p}{j}" for kind in ("y", "xp", "xm") for p in "AB"]
     for s in range(2):
         for n in range(1, half + 1):
@@ -94,7 +96,7 @@
     halves, pair, nb, wt, scale_pad, head_own, own_logit, teach_pad, teach_rows,
     acc, units_s, whole, mred, mrx, mry, nred, nrx, nry,
     part, l1_in, summed, l2_in, l3_out, l3_in, dl, loss_s,
-    grads, ra, rb, sp, sm, ry,
+    grads, ra, rb, sp, sm, ry, rq,
     send_sems, recv_sems,
 ):
     grp, sh = lax.axis_index("grp"), lax.axis_index("shard")
@@ -146,6 +148,9 @@
     halves[1] = normed[:, KH:]
     pair[c] = halves[c]
 
+    pl.semaphore_wait(barrier, len(peers))
+    send("e", halves.at[1 - c], pair.at[c], to_c)
+
     scale_pad[...] = jnp.zeros_like(scale_pad)
     scale_pad[0:2, 0:F] = gs[...]
     scale_pad[8:10, 0:F] = us[...]
@@ -161,18 +166,6 @@
 
     wt[grp] = jnp.concatenate([dequantize(gc, 0), dequantize(uc, 8)], axis=0).astype(bf16)
 
-    head_own[...] = jnp.zeros_like(head_own)
-    head_own[0:B, :] = head[:, pl.ds(pl.multiple_of(grp * RB, RB), RB)].astype(f32)
-    head_block = head_own[...].astype(bf16)
-    w_down = dequantize(dc, 16).astype(bf16)
-    product = nt(w_down, head_block)
-    rows = mred.shape[0] * mred.shape[1]
-    tail = jnp.zeros((rows - F, LANES), f32)
-    mred[...] = jnp.concatenate([product, tail], axis=0).reshape(mred.shape)
-
-    pl.semaphore_wait(barrier, len(peers))
-
-    send("e", halves.at[1 - c], pair.at[c], to_c)
     def gat(dx, j):
         return xat(dx) * Y + yat(j)
 
@@ -223,32 +216,39 @@
     def column_half(ref, at):
         return ref.at[:, pl.ds(at * (KH // 2), KH // 2)]
 
+    def one_way(s, d, q, sign):
+        return d < half or (s == 0 and (q == 0) == (sign == 1))
+
+    def next_z(s, d, q):
+        for reach in (2, 1):
+            for way, sign in (("p", 1), ("m", -1)):
+                goal = d + reach
+                if goal <= half and REACH[s][goal] == reach and one_way(s, goal, q, sign):
+                    block = column_half(block_of(s, -sign * d), q)
+                    pass_on(f"z{way}{s}{q}_{goal}", block, to_z(sign * reach))
+
     def start_z(s):
-        block = block_of(s, 0)
         for q in range(2):
             if s:
-                recv(f"hx{q}", column_half(block, q), to_h)
-            pass_on(f"zp{s}{q}_1", column_half(block, q), to_z(1))
-            pass_on(f"zm{s}{q}_1", column_half(block, q), to_z(-1))
-        pass_on(f"c{s}_0", block, to_c)
-
-    def step_z(s, n):
-        low, high = block_of(s, -n), block_of(s, n)
+                recv(f"hx{q}", column_half(block_of(s, 0), q), to_h)
+            next_z(s, 0, q)
+        pass_on(f"c{s}_0", block_of(s, 0), to_c)
+
+    def step_z(s, d):
         for q in range(2):
-            if n < half:
-                recv(f"zp{s}{q}_{n}", column_half(low, q), to_z(-1))
-                if n + 1 < half or q == 0:
-                    pass_on(f"zp{s}{q}_{n + 1}", column_half(low, q), to_z(1))
-                recv(f"zm{s}{q}_{n}", column_half(high, q), to_z(1))
-                if n + 1 < half or q == 1:
-                    pass_on(f"zm{s}{q}_{n + 1}", column_half(high, q), to_z(-1))
-            elif q == 0:
-                recv(f"zp{s}0_{n}", column_half(low, 0), to_z(-1))
-            else:
-                recv(f"zm{s}1_{n}", column_half(low, 1), to_z(1))
-        if n < half:
-            pass_on(f"c{s}_{-n}", low, to_c)
-        pass_on(f"c{s}_{n}", high, to_c)
+            block = column_half(block_of(s, half), q)
+            if s == 1 and d == half:
+                recv(f"hy{q}", block, to_h)
+            for way, sign in (("p", 1), ("m", -1)):
+                if one_way(s, d, q, sign):
+                    recv(f"z{way}{s}{q}_{d}", column_half(block_of(s, -sign * d), q), to_z(-sign * REACH[s][d]))
+            if s == 0 and d == half:
+                pass_on(f"hy{q}", block, to_h)
+            if d < half:
+                next_z(s, d, q)
+        if d < half:
+            pass_on(f"c{s}_{-d}", block_of(s, -d), to_c)
+        pass_on(f"c{s}_{d}", block_of(s, d), to_c)
 
     def sum_start(kind, red, rx):
         for k in range(1, X):
@@ -275,18 +275,26 @@
             whole[xat(-k)] = ry_[Y + k - 1]
         return whole[...].reshape(red.shape[0] * red.shape[1], LANES)[:F]
 
-    sum_start("m", mred, mrx)
-    spread_x(0)
-    start_y("A", 1)
     recv("e", pair.at[1 - c], to_c)
     nb[c, z * H + h] = pair[...].reshape(2 * T8, KH).astype(bf16)
     own = block_of(0, 0)
     for q in range(2):
         pass_on(f"hx{q}", column_half(own, q), to_h)
     start_z(0)
-    start_y("B", 1)
-    start_y("A", 2)
-    start_y("B", 2)
+    spread_x(0)
+    for j in (1, 2):
+        for p in "AB":
+            start_y(p, j)
+
+    head_own[...] = jnp.zeros_like(head_own)
+    head_own[0:B, :] = head[:, pl.ds(pl.multiple_of(grp * RB, RB), RB)].astype(f32)
+    head_block = head_own[...].astype(bf16)
+    w_down = dequantize(dc, 16).astype(bf16)
+    product = nt(w_down, head_block)
+    rows = mred.shape[0] * mred.shape[1]
+    tail = jnp.zeros((rows - F, LANES), f32)
+    mred[...] = jnp.concatenate([product, tail], axis=0).reshape(mred.shape)
+    sum_start("m", mred, mrx)
 
     step_z(0, 1)
     forward_x(0)
@@ -299,11 +307,11 @@
     step_z(0, 4)
     step_z(1, 2)
     forward_x(1)
-    sum_middle("m", mred, mrx, mry)
     step_z(0, 5)
     step_z(1, 3)
     spread_x(3)
     forward_x(2)
+    sum_middle("m", mred, mrx, mry)
     step_z(0, 6)
     step_z(1, 4)
     forward_x(3)
@@ -410,6 +418,7 @@
     acc[F : 2 * F, :] = d_units * acc[F : 2 * F, :]
     d_both = acc[...].astype(bf16)
 
+    ends = {j: ((CUT, CUT_1) if j == 1 else (0, CUT)) for j in range(Y)}
 
     def partial(dx, j):
         g = gat(dx, j)
@@ -418,65 +427,90 @@
     def slot(dx, j):
         return (dx % X) * Y + j
 
+    def piece(ref, first, last):
+        return ref.at[pl.ds(first, last - first)]
+
+    def early_rs():
+        for dx in (2, 1, -1, 0):
+            partial(dx, 1)
+            send(f"rq{dx % X}", piece(grads.at[slot(dx, 1)], 0, CUT), rq.at[dx % X], to_y(1))
+
+    def take_early(dx):
+        recv(f"rq{dx % X}", rq.at[dx % X], to_y(1))
+        at = slot(dx, 0)
+        grads[at, 0:CUT, :] = (grads[at, 0:CUT, :].astype(f32) + rq[dx % X].astype(f32)).astype(bf16)
+
+    def fill(dx, j):
+        if j != 1:
+            partial(dx, j)
+        if j == 0:
+            take_early(dx)
+
     def start_rs(j):
-        partial(2, j)
+        first, mid = ends[j]
+        fill(2, j)
         opposite = grads.at[slot(2, j)]
-        send(f"ra{j}", rows_of(opposite, "A"), ra.at[j], to_x(1))
-        send(f"rb{j}", rows_of(opposite, "B"), rb.at[j], to_x(-1))
+        send(f"ra{j}", piece(opposite, first, mid), piece(ra.at[j], 0, mid - first), to_x(1))
+        send(f"rb{j}", piece(opposite, mid, 2 * F), piece(rb.at[j], 0, 2 * F - mid), to_x(-1))
 
     def join_rs(j):
-        partial(1, j)
-        recv(f"ra{j}", ra.at[j], to_x(-1))
+        first, mid = ends[j]
+        fill(1, j)
+        recv(f"ra{j}", piece(ra.at[j], 0, mid - first), to_x(-1))
         at = slot(1, j)
-        joined = grads[at, 0:CUT, :].astype(f32) + ra[j].astype(f32)
-        grads[at, 0:CUT, :] = joined.astype(bf16)
-        send(f"sp{j}", grads.at[at], sp.at[j], to_x(1))
-        partial(-1, j)
-        recv(f"rb{j}", rb.at[j], to_x(1))
+        joined = grads[at, first:mid, :].astype(f32) + ra[j, 0 : mid - first, :].astype(f32)
+        grads[at, first:mid, :] = joined.astype(bf16)
+        send(f"sp{j}", piece(grads.at[at], first, 2 * F), piece(sp.at[j], first, 2 * F), to_x(1))
+        fill(-1, j)
+        recv(f"rb{j}", piece(rb.at[j], 0, 2 * F - mid), to_x(1))
         at = slot(-1, j)
-        joined = grads[at, CUT : 2 * F, :].astype(f32) + rb[j].astype(f32)
-        grads[at, CUT : 2 * F, :] = joined.astype(bf16)
-        send(f"sm{j}", grads.at[at], sm.at[j], to_x(-1))
-        partial(0, j)
+        joined = grads[at, mid : 2 * F, :].astype(f32) + rb[j, 0 : 2 * F - mid, :].astype(f32)
+        grads[at, mid : 2 * F, :] = joined.astype(bf16)
+        send(f"sm{j}", piece(grads.at[at], first, 2 * F), piece(sm.at[j], first, 2 * F), to_x(-1))
+        fill(0, j)
 
     def finish_rs(j):
-        recv(f"sp{j}", sp.at[j], to_x(-1))
-        recv(f"sm{j}", sm.at[j], to_x(1))
+        first, mid = ends[j]
+        recv(f"sp{j}", piece(sp.at[j], first, 2 * F), to_x(-1))
+        recv(f"sm{j}", piece(sm.at[j], first, 2 * F), to_x(1))
         at = slot(0, j)
-        total = grads[at].astype(f32) + sp[j].astype(f32) + sm[j].astype(f32)
+        rows_j = slice(first, 2 * F)
+        total = grads[at, rows_j, :].astype(f32) + sp[j, rows_j, :].astype(f32) + sm[j, rows_j, :].astype(f32)
         if j == 2:
             recv("ry3", ry.at[2], to_y(1))
             total = total + ry[2].astype(f32)
         if j == 0:
             return total
-        grads[at] = total.astype(bf16)
-        send(f"ry{j}", grads.at[at], ry.at[j - 1], to_y(2 if j == 2 else 1))
+        grads[at, rows_j, :] = total.astype(bf16)
+        send(f"ry{j}", piece(grads.at[at], first, 2 * F), piece(ry.at[j - 1], first, 2 * F), to_y(2 if j == 2 else 1))
 
     start_rs(3)
+    early_rs()
+    start_rs(2)
     product = nn(units_s[...].astype(bf16), d_logits)
     nred[...] = jnp.concatenate([product, tail], axis=0).reshape(nred.shape)
     sum_start("n", nred, nrx)
-    start_rs(2)
     join_rs(3)
     start_rs(1)
     join_rs(2)
     start_rs(0)
     finish_rs(3)
+    join_rs(1)
     sum_middle("n", nred, nrx, nry)
-    join_rs(1)
     finish_rs(2)
+    join_rs(0)
     sum_spread("n", nred, nrx, nry)
-    join_rs(0)
     finish_rs(1)
     n_high, n_low = split(sum_end("n", nred, nrx, nry))
     head_block = head_own[...].astype(bf16)
     gd_o[...] = nn(n_high, head_block) + nn(n_low, head_block)
-    result = finish_rs(0)
-    for j in (1, 2):
-        recv(f"ry{j}", ry.at[j - 1], to_y(j))
-        result = result + ry[j - 1].astype(f32)
-    gg_o[...] = result[0:F]
-    gu_o[...] = result[F : 2 * F]
+    acc[:, 0:RB] = finish_rs(0)
+    recv("ry2", ry.at[1], to_y(2))
+    acc[:, 0:RB] += ry[1].astype(f32)
+    recv("ry1", piece(ry.at[0], CUT, 2 * F), to_y(1))
+    acc[CUT : 2 * F, 0:RB] += ry[0, CUT : 2 * F, :].astype(f32)
+    gg_o[...] = acc[0:F, 0:RB]
+    gu_o[...] = acc[F : 2 * F, 0:RB]
     wires.finish()
 
 
@@ -528,6 +562,7 @@
             V((Y, 2 * F, RB), bf16),
             V((Y, 2 * F, RB), bf16),
             V((Y - 1, 2 * F, RB), bf16),
+            V((X, CUT, RB), bf16),
             pltpu.SemaphoreType.DMA((len(names),)),
             pltpu.SemaphoreType.DMA((len(names),)),
         ]

time: 111 us -> 107 us (0.964)
  Pallas kernels: 106 us -> 102 us
    pallas_call x1, Pallas kernels: 106 us -> 102 us  [local(): pl.pallas_call(functools.partial(kernel, names, Z, D, F, B), out_shape=(j...]
where the time goes in v3:
time: 107 us
  Pallas kernels  102 us (95%)
  local copies, waits for them, and re-layouts  4.43 us (4%)
    pallas_call x1, Pallas kernels, local(): pl.pallas_call(functools.partial(kernel, names, Z, D, F, B), out_shape=(j...  102 us
    unnamed x10, local copies, waits for them, and re-layouts  4.43 us

profile of v3, /device:TPU:1, one launch (start us, length us, event | category | flops | bytes accessed | tf_op | source)
XLA Modules:
  0.0 106.9 jit_solution(9136270073053108269)
XLA Ops:
  0.6 101.8 %step.1 = (f32[1,8]{1,0:T(1,128)}, f32[152,256]{1,0:T(8,128)}, f32[152,256]{1,0:T(8,128)}, f32[152,256]{1,0:T(8,128)}) custom-call(bf16[8,4096]{1,0:T(8,128)(2,1)} %hid.1, f32[1,4096]{1,0:T(1,128)} %bitcast.18, bf16[152,256]{1,0:T(8,128)(2,1)} %bitcast.15, f32[2,152]{1,0:T(2,128)} %gs.1, bf16[152,256]{1,0:T(8,128)(2,1)} %bitcast.16, f32[2,152]{1,0:T(2,128)} %us.1, ...), custom_call_target="tpu_custom_call" | custom-call | tf_op jit(solution)/shard_map/step/pallas_call | solution.py:569
  102.5 0.0 copy-start.2
  102.5 0.7 copy-done.2
  103.2 0.5 copy.19
  103.7 0.0 copy-start.1
  103.7 1.6 %copy.20 = f32[256,152]{0,1:T(8,128)} copy(f32[256,152]{0,1:T(8,128)} %bitcast.14) | data formatting | bytes 311296
  105.3 0.0 copy-done.1
  105.3 0.0 copy-start
  105.3 0.7 copy.21
  106.0 0.3 copy-done
  106.3 0.7 copy.22
Async XLA Ops:
  102.5 0.7 copy-start.2
  103.7 1.6 %copy-start.1 = (f32[152,256]{1,0:T(8,128)S(1)}, f32[152,256]{1,0:T(8,128)}, u32[]{:S(2)}) copy-start(f32[152,256]{1,0:T(8,128)} %get-tuple-element.10) | copy-start | bytes 466948
  105.3 1.0 copy-start

commit v4 on v3

--- a/solution.py
+++ b/solution.py
@@ -352,7 +352,8 @@
     part[1] = share[:, 1].reshape(Z, H, T8, LANES)
     send("l1", part.at[1 - c], l1_in, to_c)
     recv("l1", l1_in, to_c)
-    summed[...] = part[c] + l1_in[...]
+    shares = part[c] + l1_in[...]
+    summed[...] = shares.reshape(Z, H * T8, LANES).astype(bf16)
     for k in around:
         send(f"l2_{k}", summed.at[zat(k)], l2_in.at[k], to_z(k))
 
@@ -381,11 +382,11 @@
     log_teacher = log_softmax(teacher)
     p_teacher = jnp.exp(log_teacher)
 
-    total = summed[z]
+    total = summed[z].astype(f32)
     for k in reversed(around):
         recv(f"l2_{k}", l2_in.at[k], to_z(-k))
-        total = total + l2_in[k]
-    l3_out[...] = total
+        total = total + l2_in[k].astype(f32)
+    l3_out[...] = total.reshape(H, T8, LANES)
     l3_out[h] = l3_out[h] + own_logit[...]
     send("l3", l3_out, l3_in, to_h)
     acc[0:F, :] = up * sig * (1.0 + gate * (1.0 - sig))
@@ -512,6 +513,12 @@
     gg_o[...] = acc[0:F, 0:RB]
     gu_o[...] = acc[F : 2 * F, 0:RB]
     wires.finish()
+
+
+def hand_over(*refs):
+    half = len(refs) // 2
+    for taken, given in zip(refs[:half], refs[half:]):
+        given[...] = taken[...]
 
 
 def solution(mesh):
@@ -550,8 +557,8 @@
             V((X + Y, chunk, LANES), f32),
             V((C, Z, H, T8, LANES), f32),
             V((Z, H, T8, LANES), f32),
-            V((Z, H, T8, LANES), f32),
-            V((Z, H, T8, LANES), f32),
+            V((Z, H * T8, LANES), bf16),
+            V((Z, H * T8, LANES), bf16),
             V((H, T8, LANES), f32),
             V((H, T8, LANES), f32),
             V((C, Z, H * T8, LANES), bf16),
@@ -580,6 +587,15 @@
             hidden, norm_gain.reshape(1, D), gate_codes.T, gate_scales, up_codes.T, up_scales,
             down_codes.T, down_scales, head.T, teacher.T, targets,
         )
+        results = (loss, gate, up, down)
+        loss, gate, up, down = pl.pallas_call(
+            hand_over,
+            out_shape=tuple(jax.ShapeDtypeStruct(r.shape, r.dtype) for r in results),
+            in_specs=[pl.BlockSpec()] * 4,
+            out_specs=(pl.BlockSpec(),) * 4,
+            compiler_params=pltpu.CompilerParams(vmem_limit_bytes=62 << 20),
+            name="hand_over",
+        )(*results)
         return (loss.reshape(T8), gate.T, up.T, down.T)
 
     in_specs = (

time: 107 us -> 104 us (0.972)
  local copies, waits for them, and re-layouts: 4.43 us -> 0 us
    unnamed x10 -> x0, local copies, waits for them, and re-layouts: 4.43 us -> none
    pallas_call x0 -> x1, Pallas kernels: none -> 1.85 us  [local(): pl.pallas_call(hand_over, out_shape=tuple((jax.ShapeDtypeStruct(r.shape,...]
where the time goes in v4:
time: 104 us; the launch traced here: 103 us
  Pallas kernels  103 us (99%)
    pallas_call x1, Pallas kernels, local(): pl.pallas_call(functools.partial(kernel, names, Z, D, F, B), out_shape=(j...  101 us

profile of v4, /device:TPU:1, one launch (start us, length us, event | category | flops | bytes accessed | tf_op | source)
XLA Modules:
  0.0 103.4 jit_solution(8085819350087902145)
XLA Ops:
  0.6 100.9 %step.1 = (f32[1,8]{1,0:T(1,128)}, f32[152,256]{1,0:T(8,128)}, f32[152,256]{1,0:T(8,128)}, f32[152,256]{1,0:T(8,128)}) custom-call(bf16[8,4096]{1,0:T(8,128)(2,1)} %hid.1, f32[1,4096]{1,0:T(1,128)} %bitcast.15, bf16[152,256]{1,0:T(8,128)(2,1)} %bitcast.12, f32[2,152]{1,0:T(2,128)} %gs.1, bf16[152,256]{1,0:T(8,128)(2,1)} %bitcast.13, f32[2,152]{1,0:T(2,128)} %us.1, ...), custom_call_target="tpu_custom_call" | custom-call | tf_op jit(solution)/shard_map/step/pallas_call | solution.py:576
  101.6 1.9 %hand_over.1 = (f32[1,8]{1,0:T(1,128)}, f32[152,256]{1,0:T(8,128)}, f32[152,256]{1,0:T(8,128)}, f32[152,256]{1,0:T(8,128)}) custom-call(f32[1,8]{1,0:T(1,128)} %get-tuple-element.12.refs_0_, f32[152,256]{1,0:T(8,128)} %get-tuple-element.13.refs_1_, f32[152,256]{1,0:T(8,128)} %get-tuple-element.14.refs_2_, f32[152,256]{1,0:T(8,128)} %get-tuple-element.15.refs_3_), custom_call_target="tpu_custom_call" | custom-call | tf_op jit(solution)/shard_map/hand_over/pallas_call | solution.py:591

commit v5 on v4

--- a/solution.py
+++ b/solution.py
@@ -320,6 +320,7 @@
     step_z(1, 6)
     for j in range(Y):
         finish_x(j)
+    m_high, m_low = split(sum_end("m", mred, mrx, mry))
     for s in range(2):
         for k in range(-half + 1, half + 1):
             recv(f"c{s}_{k}", other_block_of(s, k), to_c)
@@ -331,23 +332,17 @@
         at = lax.rem(g, per)
         return nb[lax.div(g, per), :, :, pl.ds(pl.multiple_of(at * RB, RB), RB)].reshape(tokens, RB)
 
-    def add_blocks(at, carry):
-        total = acc[...]
-        for k in range(4):
-            total = total + nt(wt[4 * at + k], normed_columns(4 * at + k))
-        acc[...] = total
-        return carry
-
-    acc[...] = jnp.zeros_like(acc)
-    lax.fori_loop(0, X * Y // 4, add_blocks, 0)
+    total = nt(wt[0], normed_columns(0))
+    for g in range(1, X * Y):
+        total = total + nt(wt[g], normed_columns(g))
+    acc[...] = total
     gate, up = acc[0:F, :], acc[F : 2 * F, :]
     sig = jax.nn.sigmoid(gate)
     units = (gate * sig * up).astype(bf16)
     units_s[...] = units.astype(f32)
 
-    big_m = sum_end("m", mred, mrx, mry)
-    m_high, m_low = split(big_m)
-    share = (tn(units, m_high) + tn(units, m_low)).reshape(Z * H, C, T8, LANES)
+    share = tn(units, jnp.concatenate([m_high, m_low], axis=1))
+    share = (share[:, :LANES] + share[:, LANES:]).reshape(Z * H, C, T8, LANES)
     part[0] = share[:, 0].reshape(Z, H, T8, LANES)
     part[1] = share[:, 1].reshape(Z, H, T8, LANES)
     send("l1", part.at[1 - c], l1_in, to_c)
@@ -414,7 +409,8 @@
     ).reshape(tokens, LANES)
 
     d_logits = d_logits.astype(bf16)
-    d_units = nt(m_high, d_logits) + nt(m_low, d_logits)
+    d_units = nt(jnp.concatenate([m_high.astype(f32), m_low.astype(f32)], axis=0).astype(bf16), d_logits)
+    d_units = d_units[0:F] + d_units[F : 2 * F]
     acc[0:F, :] = d_units * acc[0:F, :]
     acc[F : 2 * F, :] = d_units * acc[F : 2 * F, :]
     d_both = acc[...].astype(bf16)

time: 104 us -> 102 us (0.981)
  Pallas kernels: 103 us -> 101 us
    pallas_call x1, Pallas kernels: 101 us -> 99 us  [local(): pl.pallas_call(functools.partial(kernel, names, Z, D, F, B), out_shape=(j...]
where the time goes in v5:
time: 102 us
  Pallas kernels  101 us (99%)
    pallas_call x1, Pallas kernels, local(): pl.pallas_call(functools.partial(kernel, names, Z, D, F, B), out_shape=(j...  99 us

profile of v5, /device:TPU:1, one launch (start us, length us, event | category | flops | bytes accessed | tf_op | source)
XLA Modules:
  0.0 101.5 jit_solution(406918112117370466)
XLA Ops:
  0.6 99.0 %step.1 = (f32[1,8]{1,0:T(1,128)}, f32[152,256]{1,0:T(8,128)}, f32[152,256]{1,0:T(8,128)}, f32[152,256]{1,0:T(8,128)}) custom-call(bf16[8,4096]{1,0:T(8,128)(2,1)} %hid.1, f32[1,4096]{1,0:T(1,128)} %bitcast.15, bf16[152,256]{1,0:T(8,128)(2,1)} %bitcast.12, f32[2,152]{1,0:T(2,128)} %gs.1, bf16[152,256]{1,0:T(8,128)(2,1)} %bitcast.13, f32[2,152]{1,0:T(2,128)} %us.1, ...), custom_call_target="tpu_custom_call" | custom-call | tf_op jit(solution)/shard_map/step/pallas_call | solution.py:572
  99.7 1.9 %hand_over.1 = (f32[1,8]{1,0:T(1,128)}, f32[152,256]{1,0:T(8,128)}, f32[152,256]{1,0:T(8,128)}, f32[152,256]{1,0:T(8,128)}) custom-call(f32[1,8]{1,0:T(1,128)} %get-tuple-element.12.refs_0_, f32[152,256]{1,0:T(8,128)} %get-tuple-element.13.refs_1_, f32[152,256]{1,0:T(8,128)} %get-tuple-element.14.refs_2_, f32[152,256]{1,0:T(8,128)} %get-tuple-element.15.refs_3_), custom_call_target="tpu_custom_call" | custom-call | tf_op jit(solution)/shard_map/hand_over/pallas_call | solution.py:587

commit v6 on v5

--- a/solution.py
+++ b/solution.py
@@ -321,21 +321,25 @@
     for j in range(Y):
         finish_x(j)
     m_high, m_low = split(sum_end("m", mred, mrx, mry))
+
+    tokens = acc.shape[1]
+    per = X * Y // 2
+
+    def normed_columns(g):
+        at = lax.rem(g, per)
+        return nb[lax.div(g, per), :, :, pl.ds(pl.multiple_of(at * RB, RB), RB)].reshape(tokens, RB)
+
+    def add_half(side):
+        total = nt(wt[side * per], normed_columns(side * per))
+        for k in range(1, per):
+            total = total + nt(wt[side * per + k], normed_columns(side * per + k))
+        return total
+
+    acc[...] = add_half(c)
     for s in range(2):
         for k in range(-half + 1, half + 1):
             recv(f"c{s}_{k}", other_block_of(s, k), to_c)
-
-    tokens = acc.shape[1]
-    per = X * Y // 2
-
-    def normed_columns(g):
-        at = lax.rem(g, per)
-        return nb[lax.div(g, per), :, :, pl.ds(pl.multiple_of(at * RB, RB), RB)].reshape(tokens, RB)
-
-    total = nt(wt[0], normed_columns(0))
-    for g in range(1, X * Y):
-        total = total + nt(wt[g], normed_columns(g))
-    acc[...] = total
+    acc[...] += add_half(1 - c)
     gate, up = acc[0:F, :], acc[F : 2 * F, :]
     sig = jax.nn.sigmoid(gate)
     units = (gate * sig * up).astype(bf16)

time: 102 us -> 101 us (level)
  no operation moved by 1% of the time
where the time goes in v6:
time: 101 us
  Pallas kernels  101 us (100%)
    pallas_call x1, Pallas kernels, local(): pl.pallas_call(functools.partial(kernel, names, Z, D, F, B), out_shape=(j...  98.7 us

profile of v6, /device:TPU:1, one launch (start us, length us, event | category | flops | bytes accessed | tf_op | source)
XLA Modules:
  0.0 101.2 jit_solution(10495381233553324393)
XLA Ops:
  0.6 98.7 %step.1 = (f32[1,8]{1,0:T(1,128)}, f32[152,256]{1,0:T(8,128)}, f32[152,256]{1,0:T(8,128)}, f32[152,256]{1,0:T(8,128)}) custom-call(bf16[8,4096]{1,0:T(8,128)(2,1)} %hid.1, f32[1,4096]{1,0:T(1,128)} %bitcast.15, bf16[152,256]{1,0:T(8,128)(2,1)} %bitcast.12, f32[2,152]{1,0:T(2,128)} %gs.1, bf16[152,256]{1,0:T(8,128)(2,1)} %bitcast.13, f32[2,152]{1,0:T(2,128)} %us.1, ...), custom_call_target="tpu_custom_call" | custom-call | tf_op jit(solution)/shard_map/step/pallas_call | solution.py:576
  99.3 1.9 %hand_over.1 = (f32[1,8]{1,0:T(1,128)}, f32[152,256]{1,0:T(8,128)}, f32[152,256]{1,0:T(8,128)}, f32[152,256]{1,0:T(8,128)}) custom-call(f32[1,8]{1,0:T(1,128)} %get-tuple-element.12.refs_0_, f32[152,256]{1,0:T(8,128)} %get-tuple-element.13.refs_1_, f32[152,256]{1,0:T(8,128)} %get-tuple-element.14.refs_2_, f32[152,256]{1,0:T(8,128)} %get-tuple-element.15.refs_3_), custom_call_target="tpu_custom_call" | custom-call | tf_op jit(solution)/shard_map/hand_over/pallas_call | solution.py:591
